TPU v7x, 32 devices: a whole 2x2x4 slice. The times are simulated.
32 devices in a mesh: pole: 4 (over y, x), row: 2 (over core), col: 4 (over z).
Axes of the slice: x: 2, y: 2, z: 4, core: 2. Of those that a mesh axis runs over, the one named last changes fastest.
Arguments:
- hamiltonian_panel: bfloat16 [6144, 512], P(('row', 'col'), 'pole'), may hold values from -0.005859375 to 0.005859375
- margin_panel: bfloat16 [6144, 512], P(('row', 'col'), 'pole'), may hold values from -0.0029296875 to 0.0029296875
- shifts: float32 [4, 2], P('pole'), may hold values from -2 to 2
- weights: float32 [4, 2], P('pole'), may hold values from 0.5 to 2
- pivot_inverse: float32 [4, 2, 512, 512], P('pole'), may hold values from -6 to 6
- selected_inverse: bfloat16 [4, 2, 6144, 6144], P('pole', None, 'row', 'col'), may hold values from -6 to 6
Outputs:
- inverse_column: float32 [4, 6144, 2, 512], P('pole', ('row', 'col'))
- inverse_pivot: float32 [4, 2, 512, 512], P('pole')
- density_column: float32 [6144, 512], P(('row', 'col'), 'pole')
- density_pivot: float32 [512, 512], P('pole')
All inputs are finite; a program needn't handle non-finite values.
Results may differ from a plain program's by a relative error of at most 0.0037.
Values may be sent and summed in bfloat16 or wider, within the bound.
A program may use at most 128 MiB of HBM per device.

v0:
```python
import jax
import jax.numpy as jnp
from jax import lax
from jax.sharding import PartitionSpec as P

HALVES = 2


def precise(left, right):
    return jnp.dot(left, right, precision=lax.Precision.HIGH, preferred_element_type=jnp.float32)


def gather_panel(pair):
    return lax.all_gather(pair, "pole", axis=2, tiled=True)


def factor_panel(pair, shift, inverse):
    hamiltonian_f = pair[0].astype(jnp.float32)
    margin_f = pair[1].astype(jnp.float32)
    real_part = hamiltonian_f - shift[0] * margin_f
    imag_part = -shift[1] * margin_f
    lower_real = precise(real_part, inverse[0]) - precise(imag_part, inverse[1])
    lower_imag = precise(real_part, inverse[1]) + precise(imag_part, inverse[0])
    return (lower_real.astype(jnp.bfloat16), lower_imag.astype(jnp.bfloat16))


def half_dot(left, right):
    return lax.dot_general(
        left, right, (((0,), (0,)), ((), ())), preferred_element_type=jnp.float32
    )


def body(hamiltonian_panel, margin_panel, shifts, weights, pivot_inverse, selected_inverse):
    shift = shifts[0]
    weight = weights[0]
    inverse = pivot_inverse[0]
    block_real = selected_inverse[0, 0]
    block_imag = selected_inverse[0, 1]
    n_row = lax.axis_size("row")
    n_col = lax.axis_size("col")
    n_pole = lax.axis_size("pole")
    width = inverse.shape[-1]
    part = width // HALVES
    own_pair = jnp.stack([hamiltonian_panel, margin_panel])
    order = [(n_row * c + r, r * n_col + c) for r in range(n_row) for c in range(n_col)]
    met_pair = gather_panel(lax.ppermute(own_pair, ("row", "col"), order))
    met_real, met_imag = factor_panel(met_pair, shift, inverse)
    partials = []
    for h in range(HALVES):
        cut = slice(h * part, (h + 1) * part)
        mine = jnp.concatenate([met_real[:, cut], met_imag[:, cut]], axis=1)
        rows = lax.all_gather(mine, "row", axis=0, tiled=True)
        turned = jnp.concatenate([rows[:, part:], -rows[:, :part]], axis=1)
        total = jnp.dot(block_imag, turned, preferred_element_type=jnp.float32) - jnp.dot(
            block_real, rows, preferred_element_type=jnp.float32
        )
        partials.append(total.astype(jnp.bfloat16))
    own_pair, partials[-1] = lax.optimization_barrier((own_pair, partials[-1]))
    own_real, own_imag = factor_panel(gather_panel(own_pair), shift, inverse)
    lower = jnp.concatenate([own_real, own_imag], axis=1)
    columns = []
    updates = []
    for h in range(HALVES):
        column = lax.psum_scatter(partials[h], "col", scatter_dimension=0, tiled=True).astype(
            jnp.float32
        )
        high = column.astype(jnp.bfloat16)
        low = (column - high.astype(jnp.float32)).astype(jnp.bfloat16)
        square = half_dot(lower, high) + half_dot(lower, low)
        update = jnp.stack(
            [
                square[:width, :part] - square[width:, part:],
                square[:width, part:] + square[width:, :part],
            ]
        )
        updates.append(lax.psum(update, ("row", "col")))
        columns.append(column.reshape(column.shape[0], 2, part))
    column = jnp.concatenate(columns, axis=2)
    pivot = inverse - jnp.concatenate(updates, axis=2)
    column_density = weight[0] * column[:, 0] - weight[1] * column[:, 1]
    share = width // n_pole
    pieces = column_density.reshape(-1, n_pole, share).swapaxes(0, 1).astype(jnp.bfloat16)
    column_share = jnp.sum(
        lax.all_to_all(pieces, "pole", 0, 0, tiled=True).astype(jnp.float32), axis=0
    )
    pivot_density = weight[0] * pivot[0] - weight[1] * pivot[1]
    pieces = pivot_density.reshape(n_pole, share, width).astype(jnp.bfloat16)
    pivot_share = jnp.sum(
        lax.all_to_all(pieces, "pole", 0, 0, tiled=True).astype(jnp.float32), axis=0
    )
    return (column[None], pivot[None], column_share, pivot_share)


def solution(mesh):
    return jax.shard_map(
        body,
        mesh=mesh,
        in_specs=(
            P(("row", "col"), "pole"),
            P(("row", "col"), "pole"),
            P("pole", None),
            P("pole", None),
            P("pole", None, None, None),
            P("pole", None, "row", "col"),
        ),
        out_specs=(
            P("pole", ("row", "col"), None, None),
            P("pole", None, None, None),
            P(("row", "col"), "pole"),
            P("pole", None),
        ),
        check_vma=False,
    )
```

profile of v0, /device:TPU:0, one launch (start us, length us, event | category | flops | bytes accessed | tf_op | source)
XLA Modules:
  0.0 350.2 jit_solution(6100513097827890616)
XLA Ops:
  7.2 1.1 pad_maximum_fusion.6
  8.3 0.7 collective-permute-start
  9.0 0.7 copy-done.17
  9.8 1.3 fusion.112
  11.8 42.8 %all-gather.5.cloned.1.call-done = bf16[2,768,512]{2,1,0:T(8,128)(2,1)} async-done(((bf16[2,768,128]{2,1,0:T(8,128)(2,1)}), bf16[2,768,512]{2,1,0:T(8,128)(2,1)}) %all-gather.5.cloned.1.call-update) | async-done | bytes 1572880 | tf_op jit(solution)/shard_map/all_gather | solution.py:14
  54.6 3.2 fusion.28
  57.9 2.9 fusion.26
  60.7 2.3 subtract_convert_fusion.5
  63.0 2.3 add_convert_fusion.1
  65.4 0.9 pad_maximum_fusion.5
  66.4 1.0 pad_maximum_fusion.4
  67.5 8.9 %all-gather.9.cloned.1.call-done = bf16[1536,512]{0,1:T(8,128)(2,1)} async-done(((bf16[768,512]{0,1:T(8,128)(2,1)}), bf16[1536,512]{0,1:T(8,128)(2,1)}) %all-gather.9.cloned.1.call-update) | async-done | bytes 1572880 | tf_op jit(solution)/shard_map/all_gather | solution.py:52
  76.3 9.2 %fusion = f32[512,3072]{1,0:T(8,128)S(1)} fusion(bf16[1536,512]{0,1:T(8,128)(2,1)} %all-gather.9.cloned.1.call-done, bf16[1,2,3072,1536]{3,2,1,0:T(8,128)(2,1)} %param.11), kind=kOutput, calls=%fused_computation | convolution fusion | flops 4831838208 | bytes 17301504 | tf_op jit(solution)/shard_map/dot_general | solution.py:54
  85.7 11.0 %fusion.19 = bf16[3072,512]{0,1:T(8,128)(2,1)} fusion(f32[512,3072]{1,0:T(8,128)S(1)} %fusion, bf16[1,2,3072,1536]{3,2,1,0:T(8,128)(2,1)} %param.11, bf16[1536,256]{0,1:T(8,128)(2,1)S(1)} %get-tuple-element.25, bf16[1536,256]{0,1:T(8,128)(2,1)S(1)} %get-tuple-element.24), kind=kOutput, calls=%fused_computation.20 | convolution fusion | flops 4838129664 | bytes 20447232 | tf_op jit(solution)/shard_map/dot_general | solution.py:54
  96.7 0.5 reduce-scatter.5.cloned.1.call-update
  97.5 1.6 fusion.107
  99.4 7.7 %fusion.2 = f32[512,3072]{1,0:T(8,128)S(1)} fusion(bf16[1536,512]{0,1:T(8,128)(2,1)S(1)} %copy-done.6, bf16[1,2,3072,1536]{3,2,1,0:T(8,128)(2,1)} %param.11), kind=kOutput, calls=%fused_computation.2 | convolution fusion | flops 4831838208 | bytes 17301504 | tf_op jit(solution)/shard_map/dot_general | solution.py:54
  107.1 10.6 %fusion.16 = bf16[3072,512]{0,1:T(8,128)(2,1)} fusion(f32[512,3072]{1,0:T(8,128)S(1)} %fusion.2, bf16[1,2,3072,1536]{3,2,1,0:T(8,128)(2,1)} %param.11, bf16[1536,256]{0,1:T(8,128)(2,1)S(1)} %get-tuple-element.23, bf16[1536,256]{0,1:T(8,128)(2,1)S(1)} %get-tuple-element.22), kind=kOutput, calls=%fused_computation.19 | convolution fusion | flops 4838129664 | bytes 20447232 | tf_op jit(solution)/shard_map/dot_general | solution.py:54
  117.7 11.2 %all-gather.11.cloned.1.call-done = bf16[2,768,512]{2,1,0:T(8,128)(2,1)} async-done(((bf16[2,768,128]{2,1,0:T(8,128)(2,1)}), bf16[2,768,512]{2,1,0:T(8,128)(2,1)}) %all-gather.11.cloned.1.call-update) | async-done | bytes 1572880 | tf_op jit(solution)/shard_map/all_gather | solution.py:14
  128.9 3.7 %fusion.53 = f32[768,512]{0,1:T(8,128)S(1)} fusion(f32[1,2,512,512]{3,2,1,0:T(8,128)S(1)} %copy-done, f32[]{:T(128)} %bitcast.2, bf16[2,768,512]{2,1,0:T(8,128)(2,1)} %all-gather.11.cloned.1.call-done), kind=kOutput, calls=%fused_computation.60 | convolution fusion | flops 1209532416 | bytes 4194308 | tf_op jit(solution)/shard_map/dot_general | solution.py:10
  132.6 2.3 fusion.55
  134.9 1.6 add_convert_fusion
  136.6 2.5 subtract_convert_fusion.4
  139.1 52.8 %reduce-scatter.5.cloned.1.call-done = bf16[768,512]{0,1:T(8,128)(2,1)} async-done(((bf16[3072,512]{0,1:T(8,128)(2,1)}), bf16[768,512]{0,1:T(8,128)(2,1)}) %reduce-scatter.5.cloned.1.call-update) | async-done | bytes 786448 | tf_op jit(solution)/shard_map/reduce_scatter | solution.py:64
  191.9 2.5 fusion.105
  194.4 1.0 convolution_add_fusion
  195.6 58.8 %reduce-scatter.3.cloned.1.call-done = bf16[768,512]{0,1:T(8,128)(2,1)} async-done(((bf16[3072,512]{0,1:T(8,128)(2,1)}), bf16[768,512]{0,1:T(8,128)(2,1)}) %reduce-scatter.3.cloned.1.call-update) | async-done | bytes 786448 | tf_op jit(solution)/shard_map/reduce_scatter | solution.py:64
  254.4 2.8 fusion.106
  257.2 1.0 convolution_add_fusion.1
  258.3 1.1 pad_maximum_fusion.3
  259.4 1.1 pad_maximum_fusion.2
  260.5 0.6 copy-done.18
  261.2 0.6 fusion.111
  262.5 0.5 copy-done.1
  263.0 1.1 copy-done.2
  264.2 1.8 fusion.22
  266.0 5.7 %copy.13 = f32[1,768,2,512]{3,2,1,0:T(2,128)} copy(f32[1,768,2,512]{1,3,2,0:T(8,128)} %fusion.22) | data formatting | bytes 6291456
  271.7 4.3 %fusion.40 = bf16[768,1,512]{0,2,1:T(8,128)(2,1)} fusion(f32[768,2,256]{0,2,1:T(8,128)} %copy-done.2, f32[768,2,256]{0,2,1:T(8,128)} %copy-done.1, f32[]{:T(128)} %bitcast.24, f32[]{:T(128)} %bitcast.23), kind=kLoop, calls=%fused_computation.43 | loop fusion | flops 2359296 | bytes 3932168 | tf_op jit(solution)/shard_map/convert_element_type | solution.py:82
  276.0 4.2 %all-to-all-start = ((bf16[4,768,128]{1,2,0:T(8,128)(2,1)}), bf16[4,768,128]{1,2,0:T(8,128)(2,1)}, u32[]{:S(2)}, u32[]{:S(2)}) async-start(bf16[4,768,128]{1,2,0:T(8,128)(2,1)} %bitcast.26), calls=%async_computation.2 | async-start | bytes 1572864 | tf_op jit(solution)/shard_map/all_to_all | solution.py:84
  280.2 45.3 %all-reduce.3.cloned.1.call-done = (f32[2,512,256]{2,1,0:T(8,128)}, f32[2,512,256]{2,1,0:T(8,128)}) async-done(((f32[2,512,256]{2,1,0:T(8,128)}, f32[2,512,256]{2,1,0:T(8,128)}), (f32[2,512,256]{2,1,0:T(8,128)}, f32[2,512,256]{2,1,0:T(8,128)})) %all-reduce.3.cloned.1.call-update) | async-done | bytes 2097168 | tf_op jit(solution)/shard_map/psum | solution.py:76
  325.5 2.0 maximum_subtract_fusion.1
  327.5 2.4 fusion.60
  329.9 4.3 %all-to-all-start.1 = ((bf16[4,128,512]{2,1,0:T(8,128)(2,1)}), bf16[4,128,512]{2,1,0:T(8,128)(2,1)}, u32[]{:S(2)}, u32[]{:S(2)}) async-start(bf16[4,128,512]{2,1,0:T(8,128)(2,1)} %bitcast.94), calls=%async_computation.3 | async-start | bytes 1048576 | tf_op jit(solution)/shard_map/all_to_all | solution.py:89
  334.2 1.3 convert_reduce_fusion
  335.5 0.9 copy.14
  336.4 2.9 maximum_subtract_fusion
  339.3 2.2 all-to-all-done.1
  341.5 1.8 convert_reduce_fusion.1
  (56 shorter events, 2.1 us)
Async XLA Ops:
  7.2 47.4 %all-gather.5.cloned.1.call-start = ((), (), s32[]{:S(2)}) async-start(), calls=%async_computation.4 | async-start | bytes 1966080 | tf_op jit(solution)/shard_map/all_gather | solution.py:14
  8.3 49.6 %copy-start.8 = (bf16[2,768,128]{2,1,0:T(8,128)(2,1)}, bf16[2,768,128]{2,1,0:T(8,128)(2,1)S(1)}, u32[]{:S(2)}) copy-start(bf16[2,768,128]{2,1,0:T(8,128)(2,1)S(1)} %pad_maximum_fusion.6) | copy-start | bytes 1179652
  8.3 0.7 collective-permute-start
  9.0 0.7 copy-start.17
  9.8 66.6 %all-gather.9.cloned.1.call-start = ((), (), s32[]{:S(2)}) async-start(), calls=%async_computation.7 | async-start | bytes 2359296 | tf_op jit(solution)/shard_map/all_gather | solution.py:52
  54.6 3.2 copy-start
  57.9 2.9 copy-start.4
  66.4 31.1 %all-gather.7.cloned.1.call-start = ((), (), s32[]{:S(2)}) async-start(), calls=%async_computation.5 | async-start | bytes 2359296 | tf_op jit(solution)/shard_map/all_gather | solution.py:52
  67.4 61.5 %all-gather.11.cloned.1.call-start = ((), (), s32[]{:S(2)}) async-start(), calls=%async_computation.9 | async-start | bytes 1966080 | tf_op jit(solution)/shard_map/all_gather | solution.py:14
  76.3 9.2 %copy-start.7 = (bf16[1536,512]{0,1:T(8,128)(2,1)S(1)}, bf16[1536,512]{0,1:T(8,128)(2,1)}, u32[]{:S(2)}) copy-start(bf16[1536,512]{0,1:T(8,128)(2,1)} %all-gather.9.cloned.1.call-done) | copy-start | bytes 4718596
  96.7 95.2 %reduce-scatter.5.cloned.1.call-start = ((), (), s32[]{:S(2)}) async-start(), calls=%async_computation.8 | async-start | bytes 3932160 | tf_op jit(solution)/shard_map/reduce_scatter | solution.py:64
  97.3 157.1 %reduce-scatter.3.cloned.1.call-start = ((), (), s32[]{:S(2)}) async-start(), calls=%async_computation.6 | async-start | bytes 3932160 | tf_op jit(solution)/shard_map/reduce_scatter | solution.py:64
  97.5 1.9 copy-start.6
  117.7 207.9 %all-reduce.3.cloned.1.call-start = ((), (), s32[]{:S(2)}) async-start(), calls=%async_computation.10 | async-start | bytes 4194304 | tf_op jit(solution)/shard_map/psum | solution.py:76
  128.9 3.8 %copy-start.3 = (bf16[2,768,512]{2,1,0:T(8,128)(2,1)S(1)}, bf16[2,768,512]{2,1,0:T(8,128)(2,1)}, u32[]{:S(2)}) copy-start(bf16[2,768,512]{2,1,0:T(8,128)(2,1)} %all-gather.11.cloned.1.call-done) | copy-start | bytes 4718596
  136.6 57.8 %copy-start.9 = (bf16[768,512]{0,1:T(8,128)(2,1)}, bf16[768,512]{0,1:T(8,128)(2,1)S(1)}, u32[]{:S(2)}) copy-start(bf16[768,512]{0,1:T(8,128)(2,1)S(1)} %add_convert_fusion) | copy-start | bytes 2359300
  191.9 2.5 copy-start.11
  191.9 2.5 copy-start.13
  254.4 2.8 copy-start.10
  254.4 2.8 copy-start.12
  254.4 2.8 copy-start.15
  260.5 0.7 copy-start.18
  260.5 1.2 copy-start.14
  261.2 1.2 copy-start.16
  261.9 1.1 copy-start.1
  263.0 1.1 copy-start.2
  276.0 53.9 %all-to-all-start = ((bf16[4,768,128]{1,2,0:T(8,128)(2,1)}), bf16[4,768,128]{1,2,0:T(8,128)(2,1)}, u32[]{:S(2)}, u32[]{:S(2)}) async-start(bf16[4,768,128]{1,2,0:T(8,128)(2,1)} %bitcast.26), calls=%async_computation.2 | async-start | bytes 1572864 | tf_op jit(solution)/shard_map/all_to_all | solution.py:84
  329.9 6.5 %copy-start.5 = (f32[2,512,256]{2,1,0:T(8,128)S(1)}, f32[2,512,256]{2,1,0:T(8,128)}, u32[]{:S(2)}) copy-start(f32[2,512,256]{2,1,0:T(8,128)} %get-tuple-element.16) | copy-start | bytes 3145732
  329.9 11.6 %all-to-all-start.1 = ((bf16[4,128,512]{2,1,0:T(8,128)(2,1)}), bf16[4,128,512]{2,1,0:T(8,128)(2,1)}, u32[]{:S(2)}, u32[]{:S(2)}) async-start(bf16[4,128,512]{2,1,0:T(8,128)(2,1)} %bitcast.94), calls=%async_computation.3 | async-start | bytes 1048576 | tf_op jit(solution)/shard_map/all_to_all | solution.py:89
Sparse Core Ops, SparseCore 0:
  10.4 44.1 all-gather.4
  66.5 9.7 all-gather.8
  77.9 10.9 all-gather.6
  96.8 32.0 all-gather.10
  131.6 60.2 reduce-scatter.4
  194.0 60.2 reduce-scatter.2
  260.7 64.8 all-reduce.2
where the time goes:
time: 351 us; the launch traced here: 350 us
  waiting for transfers between devices  223 us (64%)
  matrix products  66.5 us (19%)
  other arithmetic  23.8 us (7%)
  between operations  15.1 us (4%)
  local copies, waits for them, and re-layouts  12.5 us (4%)
  starting transfers between devices  9.61 us (3%)
    reduce_scatter x2, waiting for transfers between devices, body(): lax.psum_scatter(partials[h], 'col', scatter_dimension=0, tiled=True)  112 us
    all_gather x2, waiting for transfers between devices, gather_panel(): return lax.all_gather(pair, 'pole', axis=2, tiled=True)  54 us
    psum x1, waiting for transfers between devices, body(): updates.append(lax.psum(update, ('row', 'col')))  45.3 us
    dot_general x2, matrix products, body(): jnp.dot(block_imag, turned, preferred_element_type=jnp.float32)  21.5 us
    dot_general x8, matrix products, precise(): jnp.dot(left, right, precision=lax.Precision.HIGH, preferred_element_type...  20.8 us
    dot_general x2, matrix products, body(): jnp.dot(block_real, rows, preferred_element_type=jnp.float32)  16.9 us
    unnamed x40, local copies, waits for them, and re-layouts  10.5 us
    all_gather x2, waiting for transfers between devices, body(): rows = lax.all_gather(mine, 'row', axis=0, tiled=True)  8.9 us
  transfers between devices with their start and end apart: 10, of which 7 were waited for; matrix products, arithmetic and copies ran while one was open for 22% of the time, Pallas kernels for 0%

commit v1 on v0

--- a/solution.py
+++ b/solution.py
@@ -1,9 +1,38 @@
+import functools
 import jax
 import jax.numpy as jnp
 from jax import lax
 from jax.sharding import PartitionSpec as P
+from jax.lax import axis_index, axis_size, ppermute
 
 HALVES = 2
+
+
+def _resolve_bench(block_here, group_axis):
+    spare, p_next, even = (axis_size(group_axis), axis_index(group_axis), block_here.shape[2])
+    mat_out = y = block_here
+    raw_out = lax.dynamic_update_slice_in_dim(
+        jnp.zeros(
+            [i * spare if ix == 2 else i for ix, i in enumerate(block_here.shape)], block_here.dtype
+        ),
+        block_here,
+        p_next * even,
+        axis=2,
+    )
+    for tick in tuple(range(1, spare // 2 + 1)):
+        mat_out = ppermute(mat_out, group_axis, [(ix, (ix + 1) % spare) for ix in range(spare)])
+        raw_out = lax.dynamic_update_slice_in_dim(
+            raw_out, mat_out, (p_next - tick) % spare * even, axis=2
+        )
+        if 2 * tick < spare:
+            y = ppermute(y, group_axis, [(ix, (ix - 1) % spare) for ix in range(spare)])
+            raw_out = lax.dynamic_update_slice_in_dim(
+                raw_out, y, (p_next + tick) % spare * even, axis=2
+            )
+    return raw_out
+
+
+guide_case_over_axis = functools.partial(_resolve_bench, group_axis="pole")
 
 
 def precise(left, right):
@@ -11,7 +40,7 @@
 
 
 def gather_panel(pair):
-    return lax.all_gather(pair, "pole", axis=2, tiled=True)
+    return guide_case_over_axis(pair)
 
 
 def factor_panel(pair, shift, inverse):

time: 351 us -> 311 us (0.89)
  waiting for transfers between devices: 223 us -> 176 us
  starting transfers between devices: 9.61 us -> 18.5 us
  matrix products: 66.5 us -> 62.2 us
    all_gather x2 -> x0, waiting for transfers between devices: 54 us -> none  [gather_panel(): return lax.all_gather(pair, 'pole', axis=2, tiled=True)]
    reduce_scatter x2, waiting for transfers between devices: 112 us -> 62.1 us  [body(): lax.psum_scatter(partials[h], 'col', scatter_dimension=0, tiled=True)]
    ppermute x0 -> x6, waiting for transfers between devices: none -> 39.1 us  [the longest x4 29.4 us: _resolve_bench(): ppermute(mat_out, group_axis, [(ix, (ix + 1) % spare) for ix in range(spa...]
    all_gather x2, waiting for transfers between devices: 8.9 us -> 27.6 us  [body(): rows = lax.all_gather(mine, 'row', axis=0, tiled=True)]
    ppermute x0 -> x6, starting transfers between devices: none -> 8.92 us  [the longest x4 6.73 us: _resolve_bench(): ppermute(mat_out, group_axis, [(ix, (ix + 1) % spare) for ix in range(spa...]
    dot_general x8, matrix products: 20.8 us -> 16.5 us  [precise(): jnp.dot(left, right, precision=lax.Precision.HIGH, preferred_element_type...]
    unnamed x40 -> x32, local copies, waits for them, and re-layouts: 10.5 us -> 9.78 us
  transfers between devices with their start and end apart: 10 -> 14, of which waited for: 7 -> 11; matrix products, arithmetic and copies ran while one was open for 22% -> 25% of each run, Pallas kernels for 0% -> 0%
where the time goes in v1:
time: 311 us; the launch traced here: 310 us
  waiting for transfers between devices  176 us (57%)
  matrix products  62.2 us (20%)
  other arithmetic  23.8 us (8%)
  starting transfers between devices  18.5 us (6%)
  local copies, waits for them, and re-layouts  14.8 us (5%)
  between operations  14.8 us (5%)
    reduce_scatter x2, waiting for transfers between devices, body(): lax.psum_scatter(partials[h], 'col', scatter_dimension=0, tiled=True)  62.1 us
    psum x1, waiting for transfers between devices, body(): updates.append(lax.psum(update, ('row', 'col')))  45.2 us
    ppermute x4, waiting for transfers between devices, _resolve_bench(): ppermute(mat_out, group_axis, [(ix, (ix + 1) % spare) for ix in range(spa...  29.4 us
    all_gather x2, waiting for transfers between devices, body(): rows = lax.all_gather(mine, 'row', axis=0, tiled=True)  27.6 us
    dot_general x2, matrix products, body(): jnp.dot(block_imag, turned, preferred_element_type=jnp.float32)  21.5 us
    dot_general x2, matrix products, body(): jnp.dot(block_real, rows, preferred_element_type=jnp.float32)  16.9 us
    dot_general x8, matrix products, precise(): jnp.dot(left, right, precision=lax.Precision.HIGH, preferred_element_type...  16.5 us
    unnamed x32, local copies, waits for them, and re-layouts  9.78 us
  transfers between devices with their start and end apart: 14, of which 11 were waited for; matrix products, arithmetic and copies ran while one was open for 25% of the time, Pallas kernels for 0%

profile of v1, /device:TPU:0, one launch (start us, length us, event | category | flops | bytes accessed | tf_op | source)
XLA Modules:
  0.0 310.4 jit_solution(1861943087635687899)
XLA Ops:
  7.2 1.1 pad_maximum_fusion.6
  9.0 3.0 collective-permute-start.1
  13.0 5.7 %collective-permute-done.1 = bf16[2,768,128]{2,1,0:T(8,128)(2,1)S(1)} collective-permute-done((bf16[2,768,128]{2,1,0:T(8,128)(2,1)S(1)}, bf16[2,768,128]{2,1,0:T(8,128)(2,1)S(1)}, u32[]{:S(2)}, u32[]{:S(2)}) %collective-permute-start.1) | collective-permute-done | bytes 393248 | tf_op jit(solution)/shard_map/ppermute | solution.py:23
  18.7 1.1 collective-permute-start.3
  19.7 1.3 fusion.106
  22.1 2.1 collective-permute-done.2
  24.2 1.1 constant_dynamic-update-slice_fusion.5
  25.3 6.4 %collective-permute-done.3 = bf16[2,768,128]{2,1,0:T(8,128)(2,1)} collective-permute-done((bf16[2,768,128]{2,1,0:T(8,128)(2,1)S(1)}, bf16[2,768,128]{2,1,0:T(8,128)(2,1)}, u32[]{:S(2)}, u32[]{:S(2)}) %collective-permute-start.3) | collective-permute-done | bytes 393248 | tf_op jit(solution)/shard_map/ppermute | solution.py:23
  31.7 1.1 constant_dynamic-update-slice_fusion.4
  32.8 1.6 fusion.28
  34.4 1.6 fusion.26
  36.0 2.3 subtract_convert_fusion.5
  38.3 2.3 add_convert_fusion.1
  42.9 27.5 %all-gather.5.cloned.1.call-done = bf16[1536,512]{0,1:T(8,128)(2,1)} async-done(((bf16[768,512]{0,1:T(8,128)(2,1)}), bf16[1536,512]{0,1:T(8,128)(2,1)}) %all-gather.5.cloned.1.call-update) | async-done | bytes 1572880 | tf_op jit(solution)/shard_map/all_gather | solution.py:81
  70.5 9.2 %fusion = f32[512,3072]{1,0:T(8,128)S(1)} fusion(bf16[1536,512]{0,1:T(8,128)(2,1)} %all-gather.5.cloned.1.call-done, bf16[1,2,3072,1536]{3,2,1,0:T(8,128)(2,1)} %param.11), kind=kOutput, calls=%fused_computation | convolution fusion | flops 4831838208 | bytes 17301504 | tf_op jit(solution)/shard_map/dot_general | solution.py:83
  79.8 11.0 %fusion.19 = bf16[3072,512]{0,1:T(8,128)(2,1)} fusion(f32[512,3072]{1,0:T(8,128)S(1)} %fusion, bf16[1,2,3072,1536]{3,2,1,0:T(8,128)(2,1)} %param.11, bf16[1536,256]{0,1:T(8,128)(2,1)S(1)} %get-tuple-element.25, bf16[1536,256]{0,1:T(8,128)(2,1)S(1)} %get-tuple-element.24), kind=kOutput, calls=%fused_computation.20 | convolution fusion | flops 4838129664 | bytes 20447232 | tf_op jit(solution)/shard_map/dot_general | solution.py:83
  90.9 1.6 fusion.101
  92.8 7.7 %fusion.2 = f32[512,3072]{1,0:T(8,128)S(1)} fusion(bf16[1536,512]{0,1:T(8,128)(2,1)S(1)} %copy-done.4, bf16[1,2,3072,1536]{3,2,1,0:T(8,128)(2,1)} %param.11), kind=kOutput, calls=%fused_computation.2 | convolution fusion | flops 4831838208 | bytes 17301504 | tf_op jit(solution)/shard_map/dot_general | solution.py:83
  100.4 10.6 %fusion.16 = bf16[3072,512]{0,1:T(8,128)(2,1)} fusion(f32[512,3072]{1,0:T(8,128)S(1)} %fusion.2, bf16[1,2,3072,1536]{3,2,1,0:T(8,128)(2,1)} %param.11, bf16[1536,256]{0,1:T(8,128)(2,1)S(1)} %get-tuple-element.23, bf16[1536,256]{0,1:T(8,128)(2,1)S(1)} %get-tuple-element.22), kind=kOutput, calls=%fused_computation.19 | convolution fusion | flops 4838129664 | bytes 20447232 | tf_op jit(solution)/shard_map/dot_general | solution.py:83
  111.1 1.8 collective-permute-start.4
  112.9 1.2 collective-permute-start.5
  114.0 9.9 %collective-permute-done.4 = bf16[2,768,128]{2,1,0:T(8,128)(2,1)S(1)} collective-permute-done((bf16[2,768,128]{2,1,0:T(8,128)(2,1)S(1)}, bf16[2,768,128]{2,1,0:T(8,128)(2,1)S(1)}, u32[]{:S(2)}, u32[]{:S(2)}) %collective-permute-start.4) | collective-permute-done | bytes 393248 | tf_op jit(solution)/shard_map/ppermute | solution.py:23
  125.1 7.6 %collective-permute-done.5 = bf16[2,768,128]{2,1,0:T(8,128)(2,1)S(1)} collective-permute-done((bf16[2,768,128]{2,1,0:T(8,128)(2,1)S(1)}, bf16[2,768,128]{2,1,0:T(8,128)(2,1)S(1)}, u32[]{:S(2)}, u32[]{:S(2)}) %collective-permute-start.5) | collective-permute-done | bytes 393248 | tf_op jit(solution)/shard_map/ppermute | solution.py:28
  132.8 7.4 %collective-permute-done.6 = bf16[2,768,128]{2,1,0:T(8,128)(2,1)S(1)} collective-permute-done((bf16[2,768,128]{2,1,0:T(8,128)(2,1)S(1)}, bf16[2,768,128]{2,1,0:T(8,128)(2,1)S(1)}, u32[]{:S(2)}, u32[]{:S(2)}) %collective-permute-start.6) | collective-permute-done | bytes 393248 | tf_op jit(solution)/shard_map/ppermute | solution.py:23
  140.3 1.6 fusion.33
  141.9 1.6 fusion.35
  143.5 2.3 add_convert_fusion
  145.8 3.2 %subtract_convert_fusion.4 = bf16[768,512]{0,1:T(8,128)(2,1)} fusion(f32[768,512]{0,1:T(8,128)S(1)} %fusion.35, f32[1,2,512,512]{3,2,1,0:T(8,128)S(1)} %copy-done, f32[]{:T(128)} %bitcast.2, bf16[2,768,512]{2,1,0:T(8,128)(2,1)S(1)} %constant_dynamic-update-slice_fusion), kind=kOutput, calls=%fused_computation.57 | convolution fusion | flops 1210318848 | bytes 4980740 | tf_op jit(solution)/shard_map/dot_general | solution.py:39
  149.0 3.4 %reduce-scatter.5.cloned.1.call-done = bf16[768,512]{0,1:T(8,128)(2,1)} async-done(((bf16[3072,512]{0,1:T(8,128)(2,1)}), bf16[768,512]{0,1:T(8,128)(2,1)}) %reduce-scatter.5.cloned.1.call-update) | async-done | bytes 786448 | tf_op jit(solution)/shard_map/reduce_scatter | solution.py:93
  152.4 2.5 fusion.99
  154.9 1.0 convolution_add_fusion
  156.1 58.8 %reduce-scatter.3.cloned.1.call-done = bf16[768,512]{0,1:T(8,128)(2,1)} async-done(((bf16[3072,512]{0,1:T(8,128)(2,1)}), bf16[768,512]{0,1:T(8,128)(2,1)}) %reduce-scatter.3.cloned.1.call-update) | async-done | bytes 786448 | tf_op jit(solution)/shard_map/reduce_scatter | solution.py:93
  214.9 2.8 fusion.100
  218.8 1.1 pad_maximum_fusion.3
  219.9 1.1 pad_maximum_fusion.2
  223.5 1.1 copy-done.2
  224.7 1.8 fusion.22
  226.5 5.7 %copy.13 = f32[1,768,2,512]{3,2,1,0:T(2,128)} copy(f32[1,768,2,512]{1,3,2,0:T(8,128)} %fusion.22) | data formatting | bytes 6291456
  232.3 4.3 %fusion.40 = bf16[768,1,512]{0,2,1:T(8,128)(2,1)} fusion(f32[768,2,256]{0,2,1:T(8,128)} %copy-done.2, f32[768,2,256]{0,2,1:T(8,128)} %copy-done.1, f32[]{:T(128)} %bitcast.24, f32[]{:T(128)} %bitcast.23), kind=kLoop, calls=%fused_computation.43 | loop fusion | flops 2359296 | bytes 3932168 | tf_op jit(solution)/shard_map/convert_element_type | solution.py:111
  236.6 4.2 %all-to-all-start = ((bf16[4,768,128]{1,2,0:T(8,128)(2,1)}), bf16[4,768,128]{1,2,0:T(8,128)(2,1)}, u32[]{:S(2)}, u32[]{:S(2)}) async-start(bf16[4,768,128]{1,2,0:T(8,128)(2,1)} %bitcast.26), calls=%async_computation.2 | async-start | bytes 1572864 | tf_op jit(solution)/shard_map/all_to_all | solution.py:113
  240.8 45.2 %all-reduce.3.cloned.1.call-done = (f32[2,512,256]{2,1,0:T(8,128)}, f32[2,512,256]{2,1,0:T(8,128)}) async-done(((f32[2,512,256]{2,1,0:T(8,128)}, f32[2,512,256]{2,1,0:T(8,128)}), (f32[2,512,256]{2,1,0:T(8,128)}, f32[2,512,256]{2,1,0:T(8,128)})) %all-reduce.3.cloned.1.call-update) | async-done | bytes 2097168 | tf_op jit(solution)/shard_map/psum | solution.py:105
  286.0 2.0 maximum_subtract_fusion.1
  288.0 2.4 fusion.54
  290.4 4.3 %all-to-all-start.1 = ((bf16[4,128,512]{2,1,0:T(8,128)(2,1)}), bf16[4,128,512]{2,1,0:T(8,128)(2,1)}, u32[]{:S(2)}, u32[]{:S(2)}) async-start(bf16[4,128,512]{2,1,0:T(8,128)(2,1)} %bitcast.90), calls=%async_computation.3 | async-start | bytes 1048576 | tf_op jit(solution)/shard_map/all_to_all | solution.py:118
  294.6 1.3 convert_reduce_fusion
  296.8 2.9 maximum_subtract_fusion
  299.7 2.2 all-to-all-done.1
  302.0 1.8 convert_reduce_fusion.1
  (64 shorter events, 10.9 us)
Async XLA Ops:
  7.2 63.3 %all-gather.5.cloned.1.call-start = ((), (), s32[]{:S(2)}) async-start(), calls=%async_computation.6 | async-start | bytes 2359296 | tf_op jit(solution)/shard_map/all_gather | solution.py:81
  8.3 0.7 collective-permute-start
  9.0 9.7 %collective-permute-start.1 = (bf16[2,768,128]{2,1,0:T(8,128)(2,1)S(1)}, bf16[2,768,128]{2,1,0:T(8,128)(2,1)S(1)}, u32[]{:S(2)}, u32[]{:S(2)}) collective-permute-start(bf16[2,768,128]{2,1,0:T(8,128)(2,1)S(1)} %collective-permute-done), channel_id=1, source_target_pairs={{0,8},{8,16},{16,24},{24,0},{1,9},{9,17},{17,25},{25,1},{2,10},{10... | collective-permute-start | bytes 1179656 | tf_op jit(solution)/shard_map/ppermute | solution.py:23
  12.0 12.2 %collective-permute-start.2 = (bf16[2,768,128]{2,1,0:T(8,128)(2,1)S(1)}, bf16[2,768,128]{2,1,0:T(8,128)(2,1)}, u32[]{:S(2)}, u32[]{:S(2)}) collective-permute-start(bf16[2,768,128]{2,1,0:T(8,128)(2,1)S(1)} %collective-permute-done), channel_id=1, source_target_pairs={{0,24},{8,0},{16,8},{24,16},{1,25},{9,1},{17,9},{25,17},{2,26},{10... | collective-permute-start | bytes 1179656 | tf_op jit(solution)/shard_map/ppermute | solution.py:28
  18.7 13.0 %collective-permute-start.3 = (bf16[2,768,128]{2,1,0:T(8,128)(2,1)S(1)}, bf16[2,768,128]{2,1,0:T(8,128)(2,1)}, u32[]{:S(2)}, u32[]{:S(2)}) collective-permute-start(bf16[2,768,128]{2,1,0:T(8,128)(2,1)S(1)} %collective-permute-done.1), channel_id=1, source_target_pairs={{0,8},{8,16},{16,24},{24,0},{1,9},{9,17},{17,25},{25,1},{2,10},{10... | collective-permute-start | bytes 1179656 | tf_op jit(solution)/shard_map/ppermute | solution.py:23
  21.8 10.9 %copy-start = (f32[1,2,512,512]{3,2,1,0:T(8,128)S(1)}, f32[1,2,512,512]{3,2,1,0:T(8,128)}, u32[]{:S(2)}) copy-start(f32[1,2,512,512]{3,2,1,0:T(8,128)} %param.10) | copy-start | bytes 6291460
  41.7 49.2 %all-gather.3.cloned.1.call-start = ((), (), s32[]{:S(2)}) async-start(), calls=%async_computation.4 | async-start | bytes 2359296 | tf_op jit(solution)/shard_map/all_gather | solution.py:81
  42.7 109.7 %reduce-scatter.5.cloned.1.call-start = ((), (), s32[]{:S(2)}) async-start(), calls=%async_computation.7 | async-start | bytes 3932160 | tf_op jit(solution)/shard_map/reduce_scatter | solution.py:93
  70.5 9.2 %copy-start.5 = (bf16[1536,512]{0,1:T(8,128)(2,1)S(1)}, bf16[1536,512]{0,1:T(8,128)(2,1)}, u32[]{:S(2)}) copy-start(bf16[1536,512]{0,1:T(8,128)(2,1)} %all-gather.5.cloned.1.call-done) | copy-start | bytes 4718596
  90.8 124.1 %reduce-scatter.3.cloned.1.call-start = ((), (), s32[]{:S(2)}) async-start(), calls=%async_computation.5 | async-start | bytes 3932160 | tf_op jit(solution)/shard_map/reduce_scatter | solution.py:93
  90.9 1.9 copy-start.4
  111.0 175.0 %all-reduce.3.cloned.1.call-start = ((), (), s32[]{:S(2)}) async-start(), calls=%async_computation.8 | async-start | bytes 4194304 | tf_op jit(solution)/shard_map/psum | solution.py:105
  111.1 12.9 %collective-permute-start.4 = (bf16[2,768,128]{2,1,0:T(8,128)(2,1)S(1)}, bf16[2,768,128]{2,1,0:T(8,128)(2,1)S(1)}, u32[]{:S(2)}, u32[]{:S(2)}) collective-permute-start(bf16[2,768,128]{2,1,0:T(8,128)(2,1)S(1)} %pad_maximum_fusion.6), channel_id=1, source_target_pairs={{0,8},{8,16},{16,24},{24,0},{1,9},{9,17},{17,25},{25,1},{2,10},{10... | collective-permute-start | bytes 1179656 | tf_op jit(solution)/shard_map/ppermute | solution.py:23
  112.9 19.8 %collective-permute-start.5 = (bf16[2,768,128]{2,1,0:T(8,128)(2,1)S(1)}, bf16[2,768,128]{2,1,0:T(8,128)(2,1)S(1)}, u32[]{:S(2)}, u32[]{:S(2)}) collective-permute-start(bf16[2,768,128]{2,1,0:T(8,128)(2,1)S(1)} %pad_maximum_fusion.6), channel_id=1, source_target_pairs={{0,24},{8,0},{16,8},{24,16},{1,25},{9,1},{17,9},{25,17},{2,26},{10... | collective-permute-start | bytes 1179656 | tf_op jit(solution)/shard_map/ppermute | solution.py:28
  124.0 16.2 %collective-permute-start.6 = (bf16[2,768,128]{2,1,0:T(8,128)(2,1)S(1)}, bf16[2,768,128]{2,1,0:T(8,128)(2,1)S(1)}, u32[]{:S(2)}, u32[]{:S(2)}) collective-permute-start(bf16[2,768,128]{2,1,0:T(8,128)(2,1)S(1)} %collective-permute-done.4), channel_id=1, source_target_pairs={{0,8},{8,16},{16,24},{24,0},{1,9},{9,17},{17,25},{25,1},{2,10},{10... | collective-permute-start | bytes 1179656 | tf_op jit(solution)/shard_map/ppermute | solution.py:23
  145.8 9.1 %copy-start.6 = (bf16[768,512]{0,1:T(8,128)(2,1)}, bf16[768,512]{0,1:T(8,128)(2,1)S(1)}, u32[]{:S(2)}) copy-start(bf16[768,512]{0,1:T(8,128)(2,1)S(1)} %add_convert_fusion) | copy-start | bytes 2359300
  152.4 2.5 copy-start.8
  152.4 2.5 copy-start.10
  214.9 2.8 copy-start.7
  214.9 2.8 copy-start.9
  214.9 2.8 copy-start.12
  221.0 0.7 copy-start.14
  221.0 1.2 copy-start.11
  221.7 1.2 copy-start.13
  222.4 1.2 copy-start.1
  223.5 1.1 copy-start.2
  236.6 53.8 %all-to-all-start = ((bf16[4,768,128]{1,2,0:T(8,128)(2,1)}), bf16[4,768,128]{1,2,0:T(8,128)(2,1)}, u32[]{:S(2)}, u32[]{:S(2)}) async-start(bf16[4,768,128]{1,2,0:T(8,128)(2,1)} %bitcast.26), calls=%async_computation.2 | async-start | bytes 1572864 | tf_op jit(solution)/shard_map/all_to_all | solution.py:113
  290.4 6.5 %copy-start.3 = (f32[2,512,256]{2,1,0:T(8,128)S(1)}, f32[2,512,256]{2,1,0:T(8,128)}, u32[]{:S(2)}) copy-start(f32[2,512,256]{2,1,0:T(8,128)} %get-tuple-element.16) | copy-start | bytes 3145732
  290.4 11.6 %all-to-all-start.1 = ((bf16[4,128,512]{2,1,0:T(8,128)(2,1)}), bf16[4,128,512]{2,1,0:T(8,128)(2,1)}, u32[]{:S(2)}, u32[]{:S(2)}) async-start(bf16[4,128,512]{2,1,0:T(8,128)(2,1)} %bitcast.90), calls=%async_computation.3 | async-start | bytes 1048576 | tf_op jit(solution)/shard_map/all_to_all | solution.py:118
Sparse Core Ops, SparseCore 0:
  41.8 28.6 all-gather.4
  72.0 10.9 all-gather.2
  90.9 61.4 reduce-scatter.4
  154.6 60.2 reduce-scatter.2
  221.2 64.7 all-reduce.2
